TPU v7x, 32 devices: a whole 2x2x4 slice. The times are simulated.
32 devices in a mesh: graph: 8 (over z, x), feat: 4 (over y, core).
Axes of the slice: x: 2, y: 2, z: 4, core: 2. Of those that a mesh axis runs over, the one named last changes fastest.
Arguments:
- features: bfloat16 [128, 65536], P('feat', 'graph'), may hold values from -6 to 6
- w_self: bfloat16 [128, 128], replicated, may hold values from -0.5 to 0.5
- w_neigh: bfloat16 [128, 128], replicated, may hold values from -0.5 to 0.5
- bias: float32 [128], replicated, may hold values from -3 to 3
- hub_pick: int32 [16], P('graph'), may hold values from 0 to 63
- halo_send: int32 [128], P('graph'), may hold values from 0 to 63
- tile_dst: int32 [2048], P('graph'), may hold values from 0 to 63
- tile_src: int32 [2048], P('graph'), may hold values from 0 to 95, as said below
- tile_edges: int32 [2048], P('graph'), may hold values from 1 to 128, as said below
- tile_count: int32 [8], P('graph'), may hold values from 64 to 256, as said below
- edge_src: int32 [2048, 128], P('graph'), may hold values from 0 to 127
- edge_dst: int32 [2048, 128], P('graph'), may hold values from 0 to 127
Outputs:
- updated: bfloat16 [128, 65536], P('feat', 'graph')
Inputs may be any that keep to these rules, and one draw needn't show every extreme that they name: `tile_src`: A tile's source index counts into table_p: below 64 own blocks, then 16 hub blocks, then 2 * 8 halo blocks; the largest value occurs in every draw. `tile_edges`: some tile of every draw has all 128 slots live. `tile_count`: some partition of every draw has all 256 tiles live.
All inputs are finite; a program needn't handle non-finite values.
Results may differ from a plain program's by a relative error of at most 0.0015.
Values may be sent and summed in bfloat16 or wider, within the bound.
A program may use at most 64 MiB of HBM per device.

v0:
```python
import jax
import jax.numpy as jnp
from jax import lax
from jax.sharding import PartitionSpec as P

BLOCK = 128


def with_halo(block, sides, width):
    for axis, dim in sides:
        count = lax.axis_size(axis)
        forward = [(i, i + 1) for i in range(count - 1)]
        forward.append((count - 1, 0))
        backward = [(target, source) for source, target in forward]
        low = lax.ppermute(
            lax.slice_in_dim(block, block.shape[dim] - width, None, axis=dim), axis, forward
        )
        high = lax.ppermute(lax.slice_in_dim(block, 0, width, axis=dim), axis, backward)
        block = jnp.concatenate([low, block, high], axis=dim)
    return block


def shards(
    features,
    w_self,
    w_neigh,
    bias,
    hub_pick,
    halo_send,
    tile_dst,
    tile_src,
    tile_edges,
    tile_count,
    edge_src,
    edge_dst,
):
    feat_rows = features.shape[0]
    block_count = features.shape[1] // BLOCK
    halo_width = halo_send.shape[0] // 2
    blocks = features.reshape(feat_rows, block_count, BLOCK)
    hub_local = blocks[:, hub_pick, :]
    hub_rows = lax.all_gather(hub_local, "graph", axis=1, tiled=True)
    outgoing = blocks[:, halo_send, :]
    padded = with_halo(outgoing, (("graph", 1),), halo_width)
    table = jnp.concatenate(
        [blocks, hub_rows, padded[:, :halo_width], padded[:, 3 * halo_width :]], axis=1
    )
    flat_table = table.reshape(feat_rows, table.shape[1] * BLOCK)
    tile_slots = tile_dst.shape[0]
    edge_slots = edge_src.shape[1]
    live = (jnp.arange(edge_slots, dtype=jnp.int32)[None, :] < tile_edges[:, None]) & (
        jnp.arange(tile_slots, dtype=jnp.int32)[:, None] < tile_count[0]
    )
    source = tile_src[:, None] * BLOCK + edge_src
    gathered = flat_table[:, source]
    gathered = jnp.where(live[None], gathered, jnp.zeros((), jnp.bfloat16))
    one_hot = (
        (edge_dst[:, :, None] == jnp.arange(BLOCK, dtype=jnp.int32)[None, None, :])
        & live[:, :, None]
    ).astype(jnp.bfloat16)
    tile_sums = jnp.einsum("fte,teb->ftb", gathered, one_hot, preferred_element_type=jnp.float32)
    tile_degree = jnp.sum(one_hot, axis=1, dtype=jnp.float32)
    sums = jnp.zeros((feat_rows, block_count, BLOCK), jnp.float32).at[:, tile_dst, :].add(tile_sums)
    degree = jnp.zeros((block_count, BLOCK), jnp.float32).at[tile_dst, :].add(tile_degree)
    mean = (sums / jnp.maximum(degree, 1.0)[None]).astype(jnp.bfloat16)
    own_means = mean.reshape(feat_rows, block_count * BLOCK)
    feat_start = lax.axis_index("feat") * feat_rows
    self_rows = lax.dynamic_slice_in_dim(w_self, feat_start, feat_rows, 0)
    neigh_rows = lax.dynamic_slice_in_dim(w_neigh, feat_start, feat_rows, 0)
    input_piece = lax.all_gather(features, "feat", axis=0, tiled=True)
    mean_piece = lax.all_gather(own_means, "feat", axis=0, tiled=True)
    total = jnp.dot(self_rows, input_piece, preferred_element_type=jnp.float32) + jnp.dot(
        neigh_rows, mean_piece, preferred_element_type=jnp.float32
    )
    bias_rows = lax.dynamic_slice_in_dim(bias, feat_start, feat_rows, 0)
    return jax.nn.relu(total + bias_rows[:, None]).astype(jnp.bfloat16)


def solution(mesh):
    in_specs = (
        P("feat", "graph"),
        P(),
        P(),
        P(),
        P("graph"),
        P("graph"),
        P("graph"),
        P("graph"),
        P("graph"),
        P("graph"),
        P("graph", None),
        P("graph", None),
    )
    out_specs = P("feat", "graph")
    return jax.shard_map(shards, mesh=mesh, in_specs=in_specs, out_specs=out_specs, check_vma=False)
```

profile of v0, /device:TPU:0, one launch (start us, length us, event | category | flops | bytes accessed | tf_op | source)
XLA Modules:
  0.0 261.8 jit_solution(17399974321193589557)
XLA Ops:
  6.5 0.0 copy-start
  6.5 0.0 copy-start.1
  6.5 0.0 all-gather.4.cloned.1.call-start
  6.5 0.7 all-gather.4.cloned.1.call-update
  7.3 0.0 all-gather.6.cloned.1.call-start
  7.3 1.1 copy_bitcast_fusion.1
  8.4 0.7 compare_select_fusion.2
  9.1 0.6 gather_fusion.1
  9.7 3.0 %collective-permute-start = (bf16[32,8,128]{2,0,1:T(8,128)(2,1)S(1)}, bf16[32,8,128]{2,0,1:T(8,128)(2,1)S(1)}, u32[]{:S(2)}, u32[]{:S(2)}) collective-permute-start(bf16[32,8,128]{2,0,1:T(8,128)(2,1)S(1)} %get-tuple-element.5), channel_id=1, source_target_pairs={{0,4},{4,8},{8,12},{12,16},{16,20},{20,24},{24,28},{28,0},{1,5},{5... | collective-permute-start | bytes 196616 | tf_op jit(solution)/shard_map/ppermute | solution.py:15
  12.7 3.1 %collective-permute-start.1 = (bf16[32,8,128]{2,0,1:T(8,128)(2,1)S(1)}, bf16[32,8,128]{2,0,1:T(8,128)(2,1)S(1)}, u32[]{:S(2)}, u32[]{:S(2)}) collective-permute-start(bf16[32,8,128]{2,0,1:T(8,128)(2,1)S(1)} %get-tuple-element.6), channel_id=1, source_target_pairs={{4,0},{8,4},{12,8},{16,12},{20,16},{24,20},{28,24},{0,28},{5,1},{9... | collective-permute-start | bytes 196616 | tf_op jit(solution)/shard_map/ppermute | solution.py:18
  15.8 0.7 broadcast_multiply_fusion
  17.2 1.0 fusion.15
  18.2 0.8 fusion.16
  19.0 12.2 %convert_reduce_fusion = f32[256,128]{1,0:T(8,128)S(1)} fusion(s32[256,128]{1,0:T(8,128)} %param.23, pred[256,128]{1,0:T(8,128)(4,1)S(1)} %fusion.16), kind=kLoop, calls=%fused_computation.5 | loop fusion | flops 20938752 | bytes 294912 | tf_op jit(solution)/shard_map/reduce_sum | solution.py:62
  31.2 0.7 compare_select_fusion.1
  31.9 1.4 scatter_custom_fusion.1
  33.4 0.7 compare_select_fusion.3
  34.0 0.6 gather_fusion
  34.6 30.6 %all-gather = bf16[32,16,128]{2,0,1:T(8,128)(2,1)S(1)} all-gather(bf16[32,2,128]{2,0,1:T(8,128)(2,1)S(1)} %bitcast.35), channel_id=2, replica_groups=mesh['graph'=8,'feat'=4] {'graph'}, dimensions={1}, use_global_device_ids=true | all-gather | bytes 147456 | tf_op jit(solution)/shard_map/all_gather | solution.py:42
  65.2 0.1 copy.27
  65.2 0.0 copy-done.1
  65.2 0.1 copy.36
  65.3 0.0 collective-permute-done
  65.4 0.0 collective-permute-done.1
  65.4 1.0 pad_maximum_fusion
  66.4 3.0 %copy.33 = bf16[32,96,128]{0,2,1:T(8,128)(2,1)S(1)} copy(bf16[32,96,128]{2,1,0:T(8,128)(2,1)} %pad_maximum_fusion) | data formatting | bytes 1572864 | tf_op jit(solution)/shard_map/reshape | solution.py:48
  69.4 115.0 %gather_fusion.2 = bf16[32768,32]{1,0:T(8,128)(2,1)} fusion(bf16[32,12288]{0,1:T(8,128)(2,1)S(1)} %bitcast.30, s32[32768]{0:T(1024)S(1)} %fusion.15), kind=kCustom, calls=%fused_computation.2 | custom fusion | bytes 4325376 | tf_op jit(solution)/shard_map/gather | solution.py:55
  184.4 0.0 copy-start.2
  184.4 7.3 %copy.31 = bf16[256,128,32]{1,2,0:T(8,128)(2,1)S(1)} copy(bf16[256,128,32]{2,1,0:T(8,128)(2,1)} %bitcast.31) | data formatting | bytes 4194304 | tf_op jit(solution)/shard_map/gather | solution.py:55
  191.7 0.0 copy-done.2
  191.7 15.5 %fusion.2 = f32[256,32,128]{2,1,0:T(8,128)} fusion(s32[256,128]{1,0:T(8,128)S(1)} %copy-done.2, pred[256,128]{1,0:T(8,128)(4,1)S(1)} %fusion.16, bf16[256,128,32]{1,2,0:T(8,128)(2,1)S(1)} %copy.31), kind=kOutput, calls=%fused_computation.9 | convolution fusion | flops 277872640 | bytes 6455296 | tf_op jit(solution)/shard_map/fte,teb->ftb/dot_general | solution.py:61
  207.3 0.1 broadcast_in_dim.24
  207.4 0.0 copy-start.3
  207.4 22.5 %scatter_fusion = f32[32,64,128]{2,0,1:T(8,128)S(1)} fusion(f32[32,64,128]{2,0,1:T(8,128)S(1)} %broadcast_in_dim.24, s32[256]{0:T(256)S(1)} %compare_select_fusion.1, f32[256,32,128]{2,1,0:T(8,128)} %fusion.2), kind=kCustom, calls=%fused_computation.3 | custom fusion | flops 1048576 | bytes 12583936 | tf_op jit(solution)/shard_map/scatter-add | solution.py:63
  229.9 0.9 copy_bitcast_fusion
  230.7 0.0 all-gather.6.cloned.1.call-update
  230.8 0.0 copy-done.3
  230.8 0.1 dynamic_slice.11
  230.8 0.0 all-gather.4.cloned.1.call-done
  230.8 0.0 copy-done
  230.9 2.0 fusion.20
  232.9 19.3 %all-gather.6.cloned.1.call-done = bf16[128,8192]{1,0:T(8,128)(2,1)} async-done(((bf16[32,8192]{1,0:T(8,128)(2,1)}), bf16[128,8192]{1,0:T(8,128)(2,1)}) %all-gather.6.cloned.1.call-update) | async-done | bytes 2097168 | tf_op jit(solution)/shard_map/all_gather | solution.py:71
  252.1 2.8 %fusion.6 = bf16[32,8192]{1,0:T(8,128)(2,1)} fusion(f32[32,8192]{1,0:T(8,128)S(1)} %fusion.20, bf16[128,8192]{1,0:T(8,128)(2,1)} %all-gather.6.cloned.1.call-done, f32[32]{0:T(128)S(1)} %dynamic_slice.11, bf16[128,128]{1,0:T(8,128)(2,1)} %param.14, s32[]{:T(128)S(6)} %select_n.22), kind=kOutput, calls=%fused_computation.13 | convolution fusion | flops 68157440 | bytes 3678340 | tf_op jit(solution)/shard_map/dot_general | solution.py:72
  (7 shorter events, 0.1 us)
Async XLA Ops:
  6.5 224.3 %copy-start = (bf16[128,128]{1,0:T(8,128)(2,1)S(1)}, bf16[128,128]{1,0:T(8,128)(2,1)}, u32[]{:S(2)}) copy-start(bf16[128,128]{1,0:T(8,128)(2,1)} %param.13) | copy-start | bytes 98308
  6.5 58.7 %copy-start.1 = (bf16[32,8192]{1,0:T(8,128)(2,1)S(1)}, bf16[32,8192]{1,0:T(8,128)(2,1)}, u32[]{:S(2)}) copy-start(bf16[32,8192]{1,0:T(8,128)(2,1)} %param.12) | copy-start | bytes 1572868
  6.5 224.3 %all-gather.4.cloned.1.call-start = ((), (), s32[]{:S(2)}) async-start(), calls=%async_computation | async-start | bytes 2621440 | tf_op jit(solution)/shard_map/all_gather | solution.py:70
  7.3 244.9 %all-gather.6.cloned.1.call-start = ((), (), s32[]{:S(2)}) async-start(), calls=%async_computation.1 | async-start | bytes 2621440 | tf_op jit(solution)/shard_map/all_gather | solution.py:71
  9.7 55.6 %collective-permute-start = (bf16[32,8,128]{2,0,1:T(8,128)(2,1)S(1)}, bf16[32,8,128]{2,0,1:T(8,128)(2,1)S(1)}, u32[]{:S(2)}, u32[]{:S(2)}) collective-permute-start(bf16[32,8,128]{2,0,1:T(8,128)(2,1)S(1)} %get-tuple-element.5), channel_id=1, source_target_pairs={{0,4},{4,8},{8,12},{12,16},{16,20},{20,24},{24,28},{28,0},{1,5},{5... | collective-permute-start | bytes 196616 | tf_op jit(solution)/shard_map/ppermute | solution.py:15
  12.7 52.7 %collective-permute-start.1 = (bf16[32,8,128]{2,0,1:T(8,128)(2,1)S(1)}, bf16[32,8,128]{2,0,1:T(8,128)(2,1)S(1)}, u32[]{:S(2)}, u32[]{:S(2)}) collective-permute-start(bf16[32,8,128]{2,0,1:T(8,128)(2,1)S(1)} %get-tuple-element.6), channel_id=1, source_target_pairs={{4,0},{8,4},{12,8},{16,12},{20,16},{24,20},{28,24},{0,28},{5,1},{9... | collective-permute-start | bytes 196616 | tf_op jit(solution)/shard_map/ppermute | solution.py:18
  184.4 7.3 %copy-start.2 = (s32[256,128]{1,0:T(8,128)S(1)}, s32[256,128]{1,0:T(8,128)}, u32[]{:S(2)}) copy-start(s32[256,128]{1,0:T(8,128)} %param.23) | copy-start | bytes 393220
  207.4 23.4 %copy-start.3 = (f32[128]{0:T(128)S(1)}, f32[128]{0:T(128)}, u32[]{:S(2)}) copy-start(f32[128]{0:T(128)} %param.15) | copy-start | bytes 1540
Sparse Core Ops, SparseCore 0:
  8.9 25.2 all-gather.3
  230.9 21.2 all-gather.5
where the time goes:
time: 263 us; the launch traced here: 262 us
  local copies, waits for them, and re-layouts  128 us (49%)
  other arithmetic  42.5 us (16%)
  blocking collectives  30.6 us (12%)
  matrix products  20.3 us (8%)
  waiting for transfers between devices  20 us (8%)
  between operations  14.2 us (5%)
  starting transfers between devices  6.13 us (2%)
    gather x2, local copies, waits for them, and re-layouts, shards(): gathered = flat_table[:, source]  122 us
    all_gather x1, blocking collectives, shards(): hub_rows = lax.all_gather(hub_local, 'graph', axis=1, tiled=True)  30.6 us
    scatter-add x1, other arithmetic, shards(): jnp.zeros((feat_rows, block_count, BLOCK), jnp.float32).at[:, tile_dst, :]  22.5 us
    all_gather x1, waiting for transfers between devices, shards(): mean_piece = lax.all_gather(own_means, 'feat', axis=0, tiled=True)  19.3 us
    dot_general x1, matrix products, shards(): jnp.einsum('fte,teb->ftb', gathered, one_hot, preferred_element_type=jnp....  15.5 us
    reduce_sum x1, other arithmetic, shards(): tile_degree = jnp.sum(one_hot, axis=1, dtype=jnp.float32)  12.2 us
  transfers between devices with their start and end apart: 4, of which 1 were waited for; matrix products, arithmetic and copies ran while one was open for 72% of the time, Pallas kernels for 0%

commit v1 on v0

v1 whole, which is shorter than its diff:
```python
import functools

import jax
import jax.numpy as jnp
from jax import lax
from jax.experimental import pallas as pl
from jax.experimental.pallas import tpu as pltpu
from jax.sharding import PartitionSpec as P

BLOCK = 128
GROUP = 8
MESH = pl.DeviceIdType.MESH


def block_at(index):
    return pl.ds(pl.multiple_of(index * BLOCK, BLOCK), BLOCK)


def exchange_kernel(
    n,
    hub_per,
    halo,
    feat_ref,
    pick_ref,
    send_ref,
    ext_ref,
    own_blocks,
    hub_buf,
    halo_buf,
    send_sem,
    recv_sem,
):
    me = lax.axis_index("graph")
    col = lax.axis_index("feat")
    barrier = pltpu.get_barrier_semaphore()
    for k in range(1, n):
        pl.semaphore_signal(
            barrier, inc=1, device_id=(lax.rem(me + k, n), col), device_id_type=MESH
        )
    for b in range(own_blocks.shape[0]):
        own_blocks[b] = feat_ref[:, b * BLOCK : (b + 1) * BLOCK]
    for j in range(hub_per):
        hub_buf[:, j * BLOCK : (j + 1) * BLOCK] = own_blocks[pick_ref[j]]
    for j in range(2 * halo):
        halo_buf[:, j * BLOCK : (j + 1) * BLOCK] = own_blocks[send_ref[j]]
    hub_cols = hub_per * BLOCK
    halo_cols = halo * BLOCK
    own = pl.ds(pl.multiple_of(me * hub_cols, BLOCK), hub_cols)
    pl.semaphore_wait(barrier, n - 1)
    copies = []
    for side, peer in ((0, lax.rem(me + n - 1, n)), (1, lax.rem(me + 1, n))):
        start = n * hub_cols + (1 - side) * halo_cols
        copies.append(
            pltpu.make_async_remote_copy(
                src_ref=halo_buf.at[:, pl.ds(side * halo_cols, halo_cols)],
                dst_ref=ext_ref.at[:, pl.ds(start, halo_cols)],
                send_sem=send_sem.at[n + side],
                recv_sem=recv_sem.at[n + side],
                device_id=(peer, col),
                device_id_type=MESH,
            )
        )
    for k in range(1, n):
        copies.append(
            pltpu.make_async_remote_copy(
                src_ref=hub_buf,
                dst_ref=ext_ref.at[:, own],
                send_sem=send_sem.at[k],
                recv_sem=recv_sem.at[k],
                device_id=(lax.rem(me + k, n), col),
                device_id_type=MESH,
            )
        )
    for copy in copies:
        copy.start()
    ext_ref[:, own] = hub_buf[...]
    for copy in copies:
        copy.wait()


def exchange(features, hub_pick, halo_send, n):
    rows = features.shape[0]
    hub_per = hub_pick.shape[0]
    halo = halo_send.shape[0] // 2
    width = (n * hub_per + 2 * halo) * BLOCK
    vmem = pl.BlockSpec(memory_space=pltpu.VMEM)
    smem = pl.BlockSpec(memory_space=pltpu.SMEM)
    return pl.pallas_call(
        functools.partial(exchange_kernel, n, hub_per, halo),
        out_shape=jax.ShapeDtypeStruct((rows, width), jnp.bfloat16),
        in_specs=[vmem, smem, smem],
        out_specs=vmem,
        scratch_shapes=[
            pltpu.VMEM((features.shape[1] // BLOCK, rows, BLOCK), jnp.bfloat16),
            pltpu.VMEM((rows, hub_per * BLOCK), jnp.bfloat16),
            pltpu.VMEM((rows, 2 * halo * BLOCK), jnp.bfloat16),
            pltpu.SemaphoreType.DMA((n + 2,)),
            pltpu.SemaphoreType.DMA((n + 2,)),
        ],
        compiler_params=pltpu.CompilerParams(
            collective_id=0, has_side_effects=True, vmem_limit_bytes=32 * 1024 * 1024
        ),
    )(features, hub_pick, halo_send)


def aggregate_kernel(
    feat_ref,
    ext_ref,
    dst_ref,
    src_ref,
    edges_ref,
    count_ref,
    esrc_ref,
    edst_ref,
    mean_ref,
    table,
    sums,
):
    rows, nodes = feat_ref.shape
    blocks = nodes // BLOCK
    extra = ext_ref.shape[1] // BLOCK

    def unpack_own(b, carry):
        table[b] = feat_ref[:, block_at(b)].astype(jnp.float32)
        sums[b] = jnp.zeros_like(sums[b])
        return carry

    def unpack_ext(b, carry):
        table[blocks + b] = ext_ref[:, block_at(b)].astype(jnp.float32)
        return carry

    lax.fori_loop(0, blocks, unpack_own, 0, unroll=4)
    lax.fori_loop(0, extra, unpack_ext, 0, unroll=4)
    count = count_ref[0]
    lane = lax.broadcasted_iota(jnp.int32, (1, BLOCK), 1)
    node = lax.broadcasted_iota(jnp.int32, (BLOCK, BLOCK), 0)
    ones = jnp.ones((16, BLOCK), jnp.bfloat16)

    def group(g, carry):
        first = g * GROUP
        esrc = esrc_ref[pl.ds(pl.multiple_of(first, GROUP), GROUP), :]
        edst = edst_ref[pl.ds(pl.multiple_of(first, GROUP), GROUP), :]
        parts = []
        for j in range(GROUP):
            t = first + j
            live = jnp.where(t < count, edges_ref[t], 0)
            target = jnp.where(lane < live, edst[j : j + 1, :], -1)
            values = table[src_ref[t]]
            index = jnp.broadcast_to(esrc[j : j + 1, :], values.shape)
            picked = jnp.take_along_axis(values, index, axis=1, mode="promise_in_bounds")
            left = jnp.concatenate([picked.astype(jnp.bfloat16), ones], axis=0)
            hot = jnp.where(node == target, 1.0, 0.0).astype(jnp.bfloat16)
            parts.append(
                lax.dot_general(
                    left, hot, (((1,), (1,)), ((), ())), preferred_element_type=jnp.float32
                )
            )
        for j in range(GROUP):
            sums[dst_ref[first + j]] += parts[j]
        return carry

    lax.fori_loop(0, (count + GROUP - 1) // GROUP, group, 0)

    def finish(b, carry):
        total = sums[b]
        degree = jnp.maximum(total[rows : rows + 1, :], 1.0)
        mean_ref[:, block_at(b)] = (total[:rows, :] / degree).astype(jnp.bfloat16)
        return carry

    lax.fori_loop(0, blocks, finish, 0, unroll=4)


def aggregate(features, ext, tile_dst, tile_src, tile_edges, tile_count, edge_src, edge_dst):
    rows, nodes = features.shape
    blocks = nodes // BLOCK
    slots = blocks + ext.shape[1] // BLOCK
    vmem = pl.BlockSpec(memory_space=pltpu.VMEM)
    smem = pl.BlockSpec(memory_space=pltpu.SMEM)
    return pl.pallas_call(
        aggregate_kernel,
        out_shape=jax.ShapeDtypeStruct((rows, nodes), jnp.bfloat16),
        in_specs=[vmem, vmem, smem, smem, smem, smem, vmem, vmem],
        out_specs=vmem,
        scratch_shapes=[
            pltpu.VMEM((slots, rows, BLOCK), jnp.float32),
            pltpu.VMEM((blocks, rows + 16, BLOCK), jnp.float32),
        ],
        compiler_params=pltpu.CompilerParams(vmem_limit_bytes=32 * 1024 * 1024),
    )(features, ext, tile_dst, tile_src, tile_edges, tile_count, edge_src, edge_dst)


def shards(
    n,
    features,
    w_self,
    w_neigh,
    bias,
    hub_pick,
    halo_send,
    tile_dst,
    tile_src,
    tile_edges,
    tile_count,
    edge_src,
    edge_dst,
):
    feat_rows = features.shape[0]
    input_piece = lax.all_gather(features, "feat", axis=0, tiled=True)
    ext = exchange(features, hub_pick, halo_send, n)
    own_means = aggregate(
        features, ext, tile_dst, tile_src, tile_edges, tile_count, edge_src, edge_dst
    )
    feat_start = lax.axis_index("feat") * feat_rows
    self_rows = lax.dynamic_slice_in_dim(w_self, feat_start, feat_rows, 0)
    neigh_rows = lax.dynamic_slice_in_dim(w_neigh, feat_start, feat_rows, 0)
    mean_piece = lax.all_gather(own_means, "feat", axis=0, tiled=True)
    total = jnp.dot(self_rows, input_piece, preferred_element_type=jnp.float32) + jnp.dot(
        neigh_rows, mean_piece, preferred_element_type=jnp.float32
    )
    bias_rows = lax.dynamic_slice_in_dim(bias, feat_start, feat_rows, 0)
    return jax.nn.relu(total + bias_rows[:, None]).astype(jnp.bfloat16)


def solution(mesh):
    in_specs = (
        P("feat", "graph"),
        P(),
        P(),
        P(),
        P("graph"),
        P("graph"),
        P("graph"),
        P("graph"),
        P("graph"),
        P("graph"),
        P("graph", None),
        P("graph", None),
    )
    return jax.shard_map(
        functools.partial(shards, mesh.shape["graph"]),
        mesh=mesh,
        in_specs=in_specs,
        out_specs=P("feat", "graph"),
        check_vma=False,
    )
```

time: 263 us -> 70.3 us (0.27)
  local copies, waits for them, and re-layouts: 128 us -> 6.27 us
  other arithmetic: 42.5 us -> 0 us
  blocking collectives: 30.6 us -> 0 us
  Pallas kernels: 0 us -> 24.5 us
  matrix products: 20.3 us -> 4.82 us
  starting transfers between devices: 6.13 us -> 0.04 us
    gather x4 -> x0, local copies, waits for them, and re-layouts: 123 us -> none  [the longest x2 122 us: shards(): gathered = flat_table[:, source]]
    all_gather x1 -> x0, blocking collectives: 30.6 us -> none  [shards(): hub_rows = lax.all_gather(hub_local, 'graph', axis=1, tiled=True)]
    pallas_call x0 -> x2, Pallas kernels: none -> 24.5 us  [the longest x1 12.6 us: aggregate(): pl.pallas_call(aggregate_kernel, out_shape=jax.ShapeDtypeStruct((rows, no...]
    scatter-add x2 -> x0, other arithmetic: 23.9 us -> none  [the longest x1 22.5 us: shards(): jnp.zeros((feat_rows, block_count, BLOCK), jnp.float32).at[:, tile_dst, :]]
    dot_general x1 -> x0, matrix products: 15.5 us -> none  [shards(): jnp.einsum('fte,teb->ftb', gathered, one_hot, preferred_element_type=jnp....]
    reduce_sum x1 -> x0, other arithmetic: 12.2 us -> none  [shards(): tile_degree = jnp.sum(one_hot, axis=1, dtype=jnp.float32)]
    ppermute x2 -> x0, starting transfers between devices: 6.09 us -> none  [the longest x1 3.1 us: with_halo(): lax.ppermute(lax.slice_in_dim(block, 0, width, axis=dim), axis, backward)]
    unnamed x9 -> x20, local copies, waits for them, and re-layouts: 0.13 us -> 6.19 us
  transfers between devices with their start and end apart: 4 -> 2, of which waited for: 1 -> 1; matrix products, arithmetic and copies ran while one was open for 72% -> 3% of each run, Pallas kernels for 0% -> 35%
where the time goes in v1:
time: 70.3 us; the launch traced here: 70.6 us
  Pallas kernels  24.5 us (35%)
  waiting for transfers between devices  20.9 us (30%)
  between operations  14.1 us (20%)
  local copies, waits for them, and re-layouts  6.27 us (9%)
  matrix products  4.82 us (7%)
    all_gather x1, waiting for transfers between devices, shards(): mean_piece = lax.all_gather(own_means, 'feat', axis=0, tiled=True)  20.2 us
    pallas_call x1, Pallas kernels, aggregate(): pl.pallas_call(aggregate_kernel, out_shape=jax.ShapeDtypeStruct((rows, no...  12.6 us
    pallas_call x1, Pallas kernels, exchange(): pl.pallas_call(functools.partial(exchange_kernel, n, hub_per, halo), out_...  11.9 us
    unnamed x20, local copies, waits for them, and re-layouts  6.19 us
    dot_general x1, matrix products, shards(): jnp.dot(neigh_rows, mean_piece, preferred_element_type=jnp.float32)  2.82 us
    dot_general x1, matrix products, shards(): jnp.dot(self_rows, input_piece, preferred_element_type=jnp.float32)  2 us
  transfers between devices with their start and end apart: 2, of which 1 were waited for; matrix products, arithmetic and copies ran while one was open for 3% of the time, Pallas kernels for 35%

profile of v1, /device:TPU:0, one launch (start us, length us, event | category | flops | bytes accessed | tf_op | source)
XLA Modules:
  0.0 70.6 jit_solution(3502880303892020536)
XLA Ops:
  6.5 0.0 copy-start
  6.5 0.0 copy-start.9
  6.5 0.0 all-gather.3.cloned.1.call-start
  6.5 0.7 %all-gather.3.cloned.1.call-update = ((bf16[32,8192]{1,0:T(8,128)(2,1)}), bf16[128,8192]{1,0:T(8,128)(2,1)}) async-update(((), (), s32[]{:S(2)}) %all-gather.3.cloned.1.call-start, bf16[32,8192]{1,0:T(8,128)(2,1)} %feat_ref.3) | async-update | bytes 3145752
  7.3 0.0 all-gather.5.cloned.1.call-start
  8.0 0.0 copy-start.1
  8.0 1.0 %copy-done.1 = bf16[32,8192]{1,0:T(8,128)(2,1)S(1)} copy-done((bf16[32,8192]{1,0:T(8,128)(2,1)S(1)}, bf16[32,8192]{1,0:T(8,128)(2,1)}, u32[]{:S(2)}) %copy-start.1) | copy-done | bytes 524312
  9.0 0.0 copy-start.7
  9.0 0.7 copy-done.7
  9.7 0.0 copy-start.8
  9.7 0.7 copy-done.8
  10.3 11.9 %shard_map.118.ext_ref = bf16[32,4096]{1,0:T(8,128)(2,1)S(1)} custom-call(bf16[32,8192]{1,0:T(8,128)(2,1)S(1)} %copy-done.1, s32[2]{0:T(128)S(1)} %copy-done.7, s32[16]{0:T(128)S(1)} %copy-done.8), custom_call_target="tpu_custom_call" | custom-call | tf_op jit(solution)/shard_map/pallas_call | solution.py:88
  22.2 0.0 copy-start.2
  22.2 0.9 %copy-done.2 = s32[256,128]{1,0:T(8,128)S(1)} copy-done((s32[256,128]{1,0:T(8,128)S(1)}, s32[256,128]{1,0:T(8,128)}, u32[]{:S(2)}) %copy-start.2) | copy-done | bytes 131096
  23.1 0.0 copy-start.3
  23.1 0.9 %copy-done.3 = s32[256,128]{1,0:T(8,128)S(1)} copy-done((s32[256,128]{1,0:T(8,128)S(1)}, s32[256,128]{1,0:T(8,128)}, u32[]{:S(2)}) %copy-start.3) | copy-done | bytes 131096
  24.0 0.0 copy-start.4
  24.0 0.7 copy-done.4
  24.7 0.0 copy-start.5
  24.7 0.7 copy-done.5
  25.4 0.0 copy-start.6
  25.4 0.7 copy-done.6
  26.0 12.6 %shard_map.119 = bf16[32,8192]{1,0:T(8,128)(2,1)} custom-call(bf16[32,8192]{1,0:T(8,128)(2,1)S(1)} %copy-done.1, bf16[32,4096]{1,0:T(8,128)(2,1)S(1)} %shard_map.118.ext_ref, s32[256]{0:T(256)S(1)} %copy-done.4, s32[256]{0:T(256)S(1)} %copy-done.5, s32[256]{0:T(256)S(1)} %copy-done.6, s32[1]{0:T(128)S(6)} %copy.13.count_ref, s32[256,128]{1,0:T(8,128)S(1)} %copy-done.2, ...), custom_call_target="tpu_custom_call" | custom-call | tf_op jit(solution)/shard_map/pallas_call | solution.py:179
  38.6 0.0 all-gather.5.cloned.1.call-update
  38.7 0.0 copy-done.9
  38.7 0.1 dynamic_slice.11
  38.8 0.0 all-gather.3.cloned.1.call-done
  38.8 0.0 copy-done
  38.8 2.0 %fusion.4 = f32[32,8192]{1,0:T(8,128)S(1)} fusion(bf16[128,8192]{1,0:T(8,128)(2,1)} %all-gather.3.cloned.1.call-done, bf16[128,128]{1,0:T(8,128)(2,1)S(1)} %copy-done, s32[]{:T(128)S(6)} %select_n.2), kind=kOutput, calls=%fused_computation.5 | convolution fusion | flops 67108864 | bytes 3153924 | tf_op jit(solution)/shard_map/dot_general | solution.py:217
  40.8 20.2 %all-gather.5.cloned.1.call-done = bf16[128,8192]{1,0:T(8,128)(2,1)} async-done(((bf16[32,8192]{1,0:T(8,128)(2,1)}), bf16[128,8192]{1,0:T(8,128)(2,1)}) %all-gather.5.cloned.1.call-update) | async-done | bytes 2097168 | tf_op jit(solution)/shard_map/all_gather | solution.py:216
  61.0 2.8 %fusion.2 = bf16[32,8192]{1,0:T(8,128)(2,1)} fusion(f32[32,8192]{1,0:T(8,128)S(1)} %fusion.4, bf16[128,8192]{1,0:T(8,128)(2,1)} %all-gather.5.cloned.1.call-done, f32[32]{0:T(128)S(1)} %dynamic_slice.11, bf16[128,128]{1,0:T(8,128)(2,1)} %param.14, s32[]{:T(128)S(6)} %select_n.2), kind=kOutput, calls=%fused_computation.3 | convolution fusion | flops 68157440 | bytes 3678340 | tf_op jit(solution)/shard_map/dot_general | solution.py:217
Async XLA Ops:
  6.5 32.2 %copy-start = (bf16[128,128]{1,0:T(8,128)(2,1)S(1)}, bf16[128,128]{1,0:T(8,128)(2,1)}, u32[]{:S(2)}) copy-start(bf16[128,128]{1,0:T(8,128)(2,1)} %param.13) | copy-start | bytes 98308
  6.5 32.1 %copy-start.9 = (f32[128]{0:T(128)S(1)}, f32[128]{0:T(128)}, u32[]{:S(2)}) copy-start(f32[128]{0:T(128)} %param.15) | copy-start | bytes 1540
  6.5 32.2 %all-gather.3.cloned.1.call-start = ((), (), s32[]{:S(2)}) async-start(), calls=%async_computation | async-start | bytes 2621440 | tf_op jit(solution)/shard_map/all_gather | solution.py:208
  7.3 53.7 %all-gather.5.cloned.1.call-start = ((), (), s32[]{:S(2)}) async-start(), calls=%async_computation.1 | async-start | bytes 2621440 | tf_op jit(solution)/shard_map/all_gather | solution.py:216
  8.0 1.0 %copy-start.1 = (bf16[32,8192]{1,0:T(8,128)(2,1)S(1)}, bf16[32,8192]{1,0:T(8,128)(2,1)}, u32[]{:S(2)}) copy-start(bf16[32,8192]{1,0:T(8,128)(2,1)} %feat_ref.3) | copy-start | bytes 1572868
  9.0 0.7 copy-start.7
  9.7 0.7 copy-start.8
  22.2 0.9 %copy-start.2 = (s32[256,128]{1,0:T(8,128)S(1)}, s32[256,128]{1,0:T(8,128)}, u32[]{:S(2)}) copy-start(s32[256,128]{1,0:T(8,128)} %esrc_ref.1) | copy-start | bytes 393220
  23.1 0.9 %copy-start.3 = (s32[256,128]{1,0:T(8,128)S(1)}, s32[256,128]{1,0:T(8,128)}, u32[]{:S(2)}) copy-start(s32[256,128]{1,0:T(8,128)} %edst_ref.1) | copy-start | bytes 393220
  24.0 0.7 copy-start.4
  24.7 0.7 copy-start.5
  25.4 0.7 copy-start.6
Sparse Core Ops, SparseCore 0:
  8.9 25.2 all-gather.2
  38.8 22.1 all-gather.4

commit v2 on v1

v2 whole, which is shorter than its diff:
```python
import functools

import jax
import jax.numpy as jnp
from jax import lax
from jax.experimental import pallas as pl
from jax.experimental.pallas import tpu as pltpu
from jax.sharding import PartitionSpec as P

BLOCK = 128
GROUP = 8
CHUNKS = 2
MESH = pl.DeviceIdType.MESH


def block_at(index):
    return pl.ds(pl.multiple_of(index * BLOCK, BLOCK), BLOCK)


def layer_kernel(
    n,
    f,
    features,
    w_self,
    w_neigh,
    bias,
    hub_pick,
    halo_send,
    links,
    tile_src,
    tile_edges,
    tile_count,
    edge_src,
    edge_dst,
    out,
    feat,
    weight,
    bias_row,
    pick,
    send,
    link,
    src,
    edges,
    count_ref,
    esrc,
    edst,
    table,
    hub_buf,
    halo_buf,
    ext,
    running,
    means,
    joined,
    result,
    local_sem,
    send_sem,
    recv_sem,
    feat_send,
    feat_recv,
    mean_send,
    mean_recv,
    out_send,
    out_recv,
    own_sem,
):
    rows, nodes = feat.shape
    blocks = nodes // BLOCK
    total_rows = rows * f
    quarter = nodes // f
    per_quarter = quarter // BLOCK
    tiles = src.shape[0]
    hub_per = pick.shape[0]
    halo = send.shape[0] // 2
    me = lax.axis_index("graph")
    col = lax.axis_index("feat")
    high = col // 2
    low = lax.rem(col, 2)
    half = f // 2
    turns = [(a, b) for a in list(range(1, half)) + [0] for b in (0, 1) if (a, b) != (0, 0)]
    peers = [lax.rem(high + a, half) * 2 + lax.rem(low + b, 2) for a, b in turns]

    pairs = (
        (features, feat),
        (hub_pick, pick),
        (halo_send, send),
        (w_self, weight.at[:, pl.ds(0, total_rows)]),
        (w_neigh, weight.at[:, pl.ds(total_rows, total_rows)]),
        (bias, bias_row),
        (links, link),
        (tile_src, src),
        (tile_edges, edges),
        (tile_count, count_ref),
        (edge_src, esrc),
        (edge_dst, edst),
    )
    loads = [pltpu.make_async_copy(a, b, local_sem.at[i]) for i, (a, b) in enumerate(pairs)]
    for load in loads:
        load.start()
    barrier = pltpu.get_barrier_semaphore()
    for k in range(1, n):
        pl.semaphore_signal(
            barrier, inc=1, device_id=(lax.rem(me + k, n), col), device_id_type=MESH
        )
    for peer in peers:
        pl.semaphore_signal(barrier, inc=1, device_id=(me, peer), device_id_type=MESH)
    running[0] = jnp.zeros_like(running[0])
    for load in loads[:3]:
        load.wait()
    for b in range(blocks):
        table[b] = feat[:, b * BLOCK : (b + 1) * BLOCK].astype(jnp.float32)
    for j in range(2 * halo):
        halo_buf[:, j * BLOCK : (j + 1) * BLOCK] = table[send[j]].astype(jnp.bfloat16)
    for j in range(hub_per):
        hub_buf[:, j * BLOCK : (j + 1) * BLOCK] = table[pick[j]].astype(jnp.bfloat16)
    hub_cols = hub_per * BLOCK
    halo_cols = halo * BLOCK
    own_hubs = pl.ds(pl.multiple_of(me * hub_cols, BLOCK), hub_cols)
    own_rows = pl.ds(pl.multiple_of(col * rows, rows), rows)
    own_nodes = pl.ds(pl.multiple_of(col * quarter, BLOCK), quarter)
    pl.semaphore_wait(barrier, n - 1 + f - 1)

    copies = []
    for side, peer in ((0, lax.rem(me + n - 1, n)), (1, lax.rem(me + 1, n))):
        start = n * hub_cols + (1 - side) * halo_cols
        copies.append(
            pltpu.make_async_remote_copy(
                src_ref=halo_buf.at[:, pl.ds(side * halo_cols, halo_cols)],
                dst_ref=ext.at[:, pl.ds(start, halo_cols)],
                send_sem=send_sem.at[n + side],
                recv_sem=recv_sem.at[n + side],
                device_id=(peer, col),
                device_id_type=MESH,
            )
        )
    for k in range(1, n):
        copies.append(
            pltpu.make_async_remote_copy(
                src_ref=hub_buf,
                dst_ref=ext.at[:, own_hubs],
                send_sem=send_sem.at[k],
                recv_sem=recv_sem.at[k],
                device_id=(lax.rem(me + k, n), col),
                device_id_type=MESH,
            )
        )
    for copy in copies:
        copy.start()
    feat_copies = []
    for k, peer in enumerate(peers):
        feat_copies.append(
            pltpu.make_async_remote_copy(
                src_ref=feat.at[:, pl.ds(pl.multiple_of(peer * quarter, BLOCK), quarter)],
                dst_ref=joined.at[own_rows, :],
                send_sem=feat_send.at[k],
                recv_sem=feat_recv.at[k],
                device_id=(me, peer),
                device_id_type=MESH,
            )
        )
        feat_copies[-1].start()
    joined[own_rows, :] = feat[:, own_nodes]
    ext[:, own_hubs] = hub_buf[...]
    for load in loads[3:]:
        load.wait()
    for copy in copies:
        copy.wait()
    for b in range(ext.shape[1] // BLOCK):
        table[blocks + b] = ext[:, b * BLOCK : (b + 1) * BLOCK].astype(jnp.float32)

    count = count_ref[0]
    lane = lax.broadcasted_iota(jnp.int32, (1, BLOCK), 1)
    node = lax.broadcasted_iota(jnp.int32, (BLOCK, BLOCK), 0).astype(jnp.bfloat16)
    ones = jnp.ones((16, BLOCK), jnp.bfloat16)
    unit = jnp.ones((BLOCK, BLOCK), jnp.bfloat16)
    none = jnp.zeros((BLOCK, BLOCK), jnp.bfloat16)

    def group(g, carry):
        first = pl.multiple_of(g * GROUP, GROUP)
        esrc_rows = esrc[pl.ds(first, GROUP), :]
        edst_rows = edst[pl.ds(first, GROUP), :]
        parts = []
        for j in range(GROUP):
            t = first + j
            live = jnp.where(t < count, edges[t], 0)
            target = jnp.where(lane < live, edst_rows[j : j + 1, :], -1).astype(jnp.bfloat16)
            values = table[src[t]]
            index = jnp.broadcast_to(esrc_rows[j : j + 1, :], values.shape)
            picked = jnp.take_along_axis(values, index, axis=1, mode="promise_in_bounds")
            left = jnp.concatenate([picked.astype(jnp.bfloat16), ones], axis=0)
            hot = jnp.where(node == target, unit, none)
            parts.append(
                lax.dot_general(
                    left, hot, (((1,), (1,)), ((), ())), preferred_element_type=jnp.float32
                )
            )
        for j in range(GROUP):
            running[first + j + 1] = running[link[first + j]] + parts[j]
        return carry

    lax.fori_loop(0, tiles // GROUP, group, 0)

    def quarter_means(owner):
        def finish(i, carry):
            b = owner * per_quarter + i
            total = running[link[tiles + b]]
            degree = jnp.maximum(total[rows : rows + 1, :], 1.0)
            means[:, block_at(b)] = (total[:rows, :] / degree).astype(jnp.bfloat16)
            return carry

        lax.fori_loop(0, per_quarter, finish, 0, unroll=4)

    mean_rows = pl.ds(pl.multiple_of(total_rows + col * rows, rows), rows)
    mean_copies = []
    for k, peer in enumerate(peers):
        quarter_means(peer)
        mean_copies.append(
            pltpu.make_async_remote_copy(
                src_ref=means.at[:, pl.ds(pl.multiple_of(peer * quarter, BLOCK), quarter)],
                dst_ref=joined.at[mean_rows, :],
                send_sem=mean_send.at[k],
                recv_sem=mean_recv.at[k],
                device_id=(me, peer),
                device_id_type=MESH,
            )
        )
        mean_copies[-1].start()
    quarter_means(col)
    joined[mean_rows, :] = means[:, own_nodes]
    column = jnp.transpose(jnp.broadcast_to(bias_row[...], (BLOCK, total_rows)))[:, :1]
    for copy in feat_copies:
        copy.wait()
    for copy in mean_copies:
        copy.wait()
    width = quarter // CHUNKS
    out_copies = []
    own_copies = []
    for c in range(CHUNKS):
        cols = pl.ds(c * width, width)
        total = jnp.dot(weight[...], joined[:, cols], preferred_element_type=jnp.float32)
        result[:, cols] = jnp.maximum(total + column, 0.0).astype(jnp.bfloat16)
        place = pl.ds(pl.multiple_of(col * quarter + c * width, BLOCK), width)
        for k, peer in enumerate(peers):
            out_copies.append(
                pltpu.make_async_remote_copy(
                    src_ref=result.at[pl.ds(pl.multiple_of(peer * rows, rows), rows), cols],
                    dst_ref=out.at[:, place],
                    send_sem=out_send.at[c, k],
                    recv_sem=out_recv.at[c, k],
                    device_id=(me, peer),
                    device_id_type=MESH,
                )
            )
            out_copies[-1].start()
        own_copies.append(
            pltpu.make_async_copy(
                result.at[own_rows, cols], out.at[:, place], own_sem.at[c]
            )
        )
        own_copies[-1].start()
    for copy in out_copies + own_copies:
        copy.wait()


def shards(
    n,
    f,
    features,
    w_self,
    w_neigh,
    bias,
    hub_pick,
    halo_send,
    tile_dst,
    tile_src,
    tile_edges,
    tile_count,
    edge_src,
    edge_dst,
):
    rows, nodes = features.shape
    blocks = nodes // BLOCK
    tiles = tile_dst.shape[0]
    hub_per = hub_pick.shape[0]
    halo = halo_send.shape[0] // 2
    extra = n * hub_per + 2 * halo
    full = rows * f
    quarter = nodes // f
    keys = jnp.concatenate([tile_dst, jnp.arange(blocks, dtype=jnp.int32)])
    order = jnp.arange(tiles, dtype=jnp.int32)
    bound = jnp.minimum(jnp.arange(tiles + blocks, dtype=jnp.int32), tiles)
    earlier = (keys[:, None] == tile_dst[None, :]) & (order[None, :] < bound[:, None])
    links = jnp.max(jnp.where(earlier, order[None, :] + 1, 0), axis=1)
    bf16, f32, i32 = jnp.bfloat16, jnp.float32, jnp.int32
    vmem, smem, dma = pltpu.VMEM, pltpu.SMEM, pltpu.SemaphoreType.DMA
    return pl.pallas_call(
        functools.partial(layer_kernel, n, f),
        out_shape=jax.ShapeDtypeStruct((rows, nodes), bf16),
        in_specs=[pl.BlockSpec(memory_space=pl.ANY)] * 12,
        out_specs=pl.BlockSpec(memory_space=pl.ANY),
        scratch_shapes=[
            vmem((rows, nodes), bf16),
            vmem((full, 2 * full), bf16),
            vmem((1, full), f32),
            smem((hub_per,), i32),
            smem((2 * halo,), i32),
            smem((tiles + blocks,), i32),
            smem((tiles,), i32),
            smem((tiles,), i32),
            smem((1,), i32),
            vmem(edge_src.shape, i32),
            vmem(edge_dst.shape, i32),
            vmem((blocks + extra, rows, BLOCK), f32),
            vmem((rows, hub_per * BLOCK), bf16),
            vmem((rows, 2 * halo * BLOCK), bf16),
            vmem((rows, extra * BLOCK), bf16),
            vmem((tiles + 1, rows + 16, BLOCK), f32),
            vmem((rows, nodes), bf16),
            vmem((2 * full, quarter), bf16),
            vmem((full, quarter), bf16),
            dma((12,)),
            dma((n + 2,)),
            dma((n + 2,)),
            dma((f,)),
            dma((f,)),
            dma((f,)),
            dma((f,)),
            dma((CHUNKS, f)),
            dma((CHUNKS, f)),
            dma((CHUNKS,)),
        ],
        compiler_params=pltpu.CompilerParams(
            collective_id=0, has_side_effects=True, vmem_limit_bytes=56 * 1024 * 1024
        ),
    )(
        features,
        w_self,
        w_neigh,
        bias.reshape(1, full),
        hub_pick,
        halo_send,
        links,
        tile_src,
        tile_edges,
        tile_count,
        edge_src,
        edge_dst,
    )


def solution(mesh):
    in_specs = (
        P("feat", "graph"),
        P(),
        P(),
        P(),
        P("graph"),
        P("graph"),
        P("graph"),
        P("graph"),
        P("graph"),
        P("graph"),
        P("graph", None),
        P("graph", None),
    )
    return jax.shard_map(
        functools.partial(shards, mesh.shape["graph"], mesh.shape["feat"]),
        mesh=mesh,
        in_specs=in_specs,
        out_specs=P("feat", "graph"),
        check_vma=False,
    )
```

time: 70.3 us -> 40.5 us (0.58); the launches traced: 70.6 us -> 40 us
  waiting for transfers between devices: 20.9 us -> 0 us
  between operations: 14.1 us -> 0.68 us
  Pallas kernels: 24.5 us -> 35.9 us
  matrix products: 4.82 us -> 0 us
  local copies, waits for them, and re-layouts: 6.27 us -> 2.54 us
  other arithmetic: 0 us -> 0.84 us
    all_gather x2 -> x0, waiting for transfers between devices: 20.2 us -> none  [the longest x1 20.2 us: shards(): mean_piece = lax.all_gather(own_means, 'feat', axis=0, tiled=True)]
    pallas_call x2 -> x1, Pallas kernels: 24.5 us -> 35.9 us  [shards(): pl.pallas_call(functools.partial(layer_kernel, n, f), out_shape=jax.Shape...]
    dot_general x2 -> x0, matrix products: 4.82 us -> none  [the longest x1 2.82 us: shards(): jnp.dot(neigh_rows, mean_piece, preferred_element_type=jnp.float32)]
    unnamed x20 -> x3, local copies, waits for them, and re-layouts: 6.19 us -> 2.53 us
    reduce_max x0 -> x1, other arithmetic: none -> 0.83 us  [shards(): links = jnp.max(jnp.where(earlier, order[None, :] + 1, 0), axis=1)]
    unnamed x2 -> x0, waiting for transfers between devices: 0.73 us -> none
  transfers between devices with their start and end apart: 2 -> 0, of which waited for: 1 -> 0; matrix products, arithmetic and copies ran while one was open for 3% -> 0% of each run, Pallas kernels for 35% -> 0%
where the time goes in v2:
time: 40.5 us; the launch traced here: 40 us
  Pallas kernels  35.9 us (89%)
  local copies, waits for them, and re-layouts  2.54 us (6%)
  other arithmetic  0.84 us (2%)
  between operations  0.68 us (2%)
    pallas_call x1, Pallas kernels, shards(): pl.pallas_call(functools.partial(layer_kernel, n, f), out_shape=jax.Shape...  35.9 us
    unnamed x3, local copies, waits for them, and re-layouts  2.53 us
    reduce_max x1, other arithmetic, shards(): links = jnp.max(jnp.where(earlier, order[None, :] + 1, 0), axis=1)  0.83 us

profile of v2, /device:TPU:0, one launch (start us, length us, event | category | flops | bytes accessed | tf_op | source)
XLA Modules:
  0.0 40.0 jit_solution(16877304238612453721)
XLA Ops:
  0.7 0.0 copy-start
  0.7 0.7 %copy-done = s32[256]{0:T(256)S(1)} copy-done((s32[256]{0:T(256)S(1)}, s32[256]{0:T(256)}, u32[]{:S(2)}) %copy-start) | copy-done | bytes 1048
  1.4 0.8 %select_reduce_fusion.links = s32[320]{0:T(512)} fusion(s32[256]{0:T(256)S(1)} %iota_add_fusion, s32[320]{0:T(512)S(1)} %get-tuple-element.6, s32[256]{0:T(256)S(1)} %copy-done, s32[320]{0:T(512)S(1)} %get-tuple-element.5), kind=kLoop, calls=%fused_computation | loop fusion | flops 409280 | bytes 5888 | tf_op jit(solution)/shard_map/reduce_max | solution.py:292
  2.2 35.9 %shard_map.118 = bf16[32,8192]{1,0:T(8,128)(2,1)} custom-call(bf16[32,8192]{1,0:T(8,128)(2,1)} %features.1, bf16[128,128]{1,0:T(8,128)(2,1)} %w_self.1, bf16[128,128]{1,0:T(8,128)(2,1)} %w_neigh.1, f32[1,128]{1,0:T(1,128)} %bitcast.1, s32[2]{0:T(128)} %hub_pick.1, s32[16]{0:T(128)} %halo_send.1, s32[320]{0:T(512)} %select_reduce_fusion.links, s32[256]{0:T(256)} %tile_src.1, ...), custom_call_target="tpu_custom_call" | custom-call | tf_op jit(solution)/shard_map/pallas_call | solution.py:295
  38.1 1.9 %copy.15 = bf16[32,8192]{1,0:T(8,128)(2,1)} copy(bf16[32,8192]{1,0:T(8,128)(2,1)} %shard_map.118) | data formatting | bytes 1048576
  (3 shorter events, 0.0 us)
Async XLA Ops:
  0.7 0.7 %copy-start = (s32[256]{0:T(256)S(1)}, s32[256]{0:T(256)}, u32[]{:S(2)}) copy-start(s32[256]{0:T(256)} %param.18) | copy-start | bytes 3076

commit v3 on v2

--- a/solution.py
+++ b/solution.py
@@ -26,7 +26,7 @@
     bias,
     hub_pick,
     halo_send,
-    links,
+    tile_dst,
     tile_src,
     tile_edges,
     tile_count,
@@ -38,12 +38,16 @@
     bias_row,
     pick,
     send,
-    link,
+    dst,
     src,
     edges,
     count_ref,
     esrc,
     edst,
+    link_rows,
+    link,
+    columns,
+    hot,
     table,
     hub_buf,
     halo_buf,
@@ -86,7 +90,7 @@
         (w_self, weight.at[:, pl.ds(0, total_rows)]),
         (w_neigh, weight.at[:, pl.ds(total_rows, total_rows)]),
         (bias, bias_row),
-        (links, link),
+        (tile_dst, dst),
         (tile_src, src),
         (tile_edges, edges),
         (tile_count, count_ref),
@@ -162,39 +166,71 @@
     ext[:, own_hubs] = hub_buf[...]
     for load in loads[3:]:
         load.wait()
+
+    count = count_ref[0]
+    square = (BLOCK, BLOCK)
+    lane = lax.broadcasted_iota(jnp.int32, square, 1).astype(jnp.float32)
+    sub = lax.broadcasted_iota(jnp.int32, square, 0).astype(jnp.float32)
+    spans = tiles // BLOCK
+    tile = lax.broadcasted_iota(jnp.int32, square, 1)
+    row = lax.broadcasted_iota(jnp.int32, square, 0)
+    keys = [dst[i : i + 1, :] for i in range(spans)]
+    best = [jnp.zeros((1, BLOCK), jnp.int32) for _ in range(spans + 1)]
+    for i in range(spans):
+        spread = jnp.transpose(jnp.broadcast_to(keys[i], square))
+        place = row + (i * BLOCK + 1)
+        for j in range(i, spans):
+            found = spread == keys[j]
+            if i == j:
+                found = found & (row < tile)
+            best[j] = jnp.maximum(
+                best[j], jnp.max(jnp.where(found, place, 0), axis=0, keepdims=True)
+            )
+        best[spans] = jnp.maximum(
+            best[spans], jnp.max(jnp.where(spread == tile, place, 0), axis=0, keepdims=True)
+        )
+    link_rows[...] = jnp.zeros_like(link_rows)
+    for i in range(spans + 1):
+        link_rows[i : i + 1, :] = best[i]
+    link_load = pltpu.make_async_copy(link_rows, link, local_sem.at[12])
+    link_load.start()
+    for i in range(spans):
+        order = lax.broadcasted_iota(jnp.int32, (1, BLOCK), 1) + i * BLOCK
+        live = jnp.where(order < count, edges[i : i + 1, :], 0).astype(jnp.float32)
+        target = jnp.transpose(edst[i * BLOCK : (i + 1) * BLOCK, :].astype(jnp.float32))
+        target = jnp.where(sub < live, target, -1.0)
+        for k in range(BLOCK // GROUP):
+            columns[i * (BLOCK // GROUP) + k] = target[:, k * GROUP : (k + 1) * GROUP]
+
+    def build(g, carry):
+        column = columns[g]
+        for j in range(GROUP):
+            match = jnp.broadcast_to(column[:, j : j + 1], square) == lane
+            hot[g * GROUP + j] = jnp.where(match, 1.0, 0.0).astype(jnp.bfloat16)
+        return carry
+
+    lax.fori_loop(0, tiles // GROUP, build, 0)
+    link_load.wait()
     for copy in copies:
         copy.wait()
     for b in range(ext.shape[1] // BLOCK):
         table[blocks + b] = ext[:, b * BLOCK : (b + 1) * BLOCK].astype(jnp.float32)
-
-    count = count_ref[0]
-    lane = lax.broadcasted_iota(jnp.int32, (1, BLOCK), 1)
-    node = lax.broadcasted_iota(jnp.int32, (BLOCK, BLOCK), 0).astype(jnp.bfloat16)
     ones = jnp.ones((16, BLOCK), jnp.bfloat16)
-    unit = jnp.ones((BLOCK, BLOCK), jnp.bfloat16)
-    none = jnp.zeros((BLOCK, BLOCK), jnp.bfloat16)
 
     def group(g, carry):
         first = pl.multiple_of(g * GROUP, GROUP)
         esrc_rows = esrc[pl.ds(first, GROUP), :]
-        edst_rows = edst[pl.ds(first, GROUP), :]
         parts = []
         for j in range(GROUP):
-            t = first + j
-            live = jnp.where(t < count, edges[t], 0)
-            target = jnp.where(lane < live, edst_rows[j : j + 1, :], -1).astype(jnp.bfloat16)
-            values = table[src[t]]
+            values = table[src[first + j]]
             index = jnp.broadcast_to(esrc_rows[j : j + 1, :], values.shape)
             picked = jnp.take_along_axis(values, index, axis=1, mode="promise_in_bounds")
             left = jnp.concatenate([picked.astype(jnp.bfloat16), ones], axis=0)
-            hot = jnp.where(node == target, unit, none)
-            parts.append(
-                lax.dot_general(
-                    left, hot, (((1,), (1,)), ((), ())), preferred_element_type=jnp.float32
-                )
-            )
+            parts.append(jnp.dot(left, hot[first + j], preferred_element_type=jnp.float32))
+        span = g // (BLOCK // GROUP)
+        spot = lax.rem(g, BLOCK // GROUP) * GROUP
         for j in range(GROUP):
-            running[first + j + 1] = running[link[first + j]] + parts[j]
+            running[first + j + 1] = running[link[span, spot + j]] + parts[j]
         return carry
 
     lax.fori_loop(0, tiles // GROUP, group, 0)
@@ -202,7 +238,7 @@
     def quarter_means(owner):
         def finish(i, carry):
             b = owner * per_quarter + i
-            total = running[link[tiles + b]]
+            total = running[link[spans, b]]
             degree = jnp.maximum(total[rows : rows + 1, :], 1.0)
             means[:, block_at(b)] = (total[:rows, :] / degree).astype(jnp.bfloat16)
             return carry
@@ -280,16 +316,12 @@
     rows, nodes = features.shape
     blocks = nodes // BLOCK
     tiles = tile_dst.shape[0]
+    spans = tiles // BLOCK
     hub_per = hub_pick.shape[0]
     halo = halo_send.shape[0] // 2
     extra = n * hub_per + 2 * halo
     full = rows * f
     quarter = nodes // f
-    keys = jnp.concatenate([tile_dst, jnp.arange(blocks, dtype=jnp.int32)])
-    order = jnp.arange(tiles, dtype=jnp.int32)
-    bound = jnp.minimum(jnp.arange(tiles + blocks, dtype=jnp.int32), tiles)
-    earlier = (keys[:, None] == tile_dst[None, :]) & (order[None, :] < bound[:, None])
-    links = jnp.max(jnp.where(earlier, order[None, :] + 1, 0), axis=1)
     bf16, f32, i32 = jnp.bfloat16, jnp.float32, jnp.int32
     vmem, smem, dma = pltpu.VMEM, pltpu.SMEM, pltpu.SemaphoreType.DMA
     return pl.pallas_call(
@@ -303,12 +335,16 @@
             vmem((1, full), f32),
             smem((hub_per,), i32),
             smem((2 * halo,), i32),
-            smem((tiles + blocks,), i32),
+            vmem((spans, BLOCK), i32),
             smem((tiles,), i32),
-            smem((tiles,), i32),
+            vmem((spans, BLOCK), i32),
             smem((1,), i32),
             vmem(edge_src.shape, i32),
             vmem(edge_dst.shape, i32),
+            vmem((8, BLOCK), i32),
+            smem((8, BLOCK), i32),
+            vmem((tiles // GROUP, BLOCK, GROUP), f32),
+            vmem((tiles, BLOCK, BLOCK), bf16),
             vmem((blocks + extra, rows, BLOCK), f32),
             vmem((rows, hub_per * BLOCK), bf16),
             vmem((rows, 2 * halo * BLOCK), bf16),
@@ -317,7 +353,7 @@
             vmem((rows, nodes), bf16),
             vmem((2 * full, quarter), bf16),
             vmem((full, quarter), bf16),
-            dma((12,)),
+            dma((13,)),
             dma((n + 2,)),
             dma((n + 2,)),
             dma((f,)),
@@ -338,9 +374,9 @@
         bias.reshape(1, full),
         hub_pick,
         halo_send,
-        links,
+        tile_dst.reshape(spans, BLOCK),
         tile_src,
-        tile_edges,
+        tile_edges.reshape(spans, BLOCK),
         tile_count,
         edge_src,
         edge_dst,

time: 40.5 us -> 40.9 us (level)
  Pallas kernels: 35.9 us -> 38.2 us
  other arithmetic: 0.84 us -> 0 us
  local copies, waits for them, and re-layouts: 2.54 us -> 1.87 us
    pallas_call x1, Pallas kernels: 35.9 us -> 38.2 us  [shards(): pl.pallas_call(functools.partial(layer_kernel, n, f), out_shape=jax.Shape...]
    reduce_max x1 -> x0, other arithmetic: 0.83 us -> none  [shards(): links = jnp.max(jnp.where(earlier, order[None, :] + 1, 0), axis=1)]
    unnamed x3 -> x1, local copies, waits for them, and re-layouts: 2.53 us -> 1.87 us
where the time goes in v3:
time: 40.9 us; the launch traced here: 40.7 us
  Pallas kernels  38.2 us (93%)
  local copies, waits for them, and re-layouts  1.87 us (5%)
  between operations  0.66 us (2%)
    pallas_call x1, Pallas kernels, shards(): pl.pallas_call(functools.partial(layer_kernel, n, f), out_shape=jax.Shape...  38.2 us
    unnamed x1, local copies, waits for them, and re-layouts  1.87 us

profile of v3, /device:TPU:0, one launch (start us, length us, event | category | flops | bytes accessed | tf_op | source)
XLA Modules:
  0.0 40.7 jit_solution(1751557650988741192)
XLA Ops:
  0.7 38.2 %shard_map.118 = bf16[32,8192]{1,0:T(8,128)(2,1)} custom-call(bf16[32,8192]{1,0:T(8,128)(2,1)} %features.1, bf16[128,128]{1,0:T(8,128)(2,1)} %w_self.1, bf16[128,128]{1,0:T(8,128)(2,1)} %w_neigh.1, f32[1,128]{1,0:T(1,128)} %bitcast.5, s32[2]{0:T(128)} %hub_pick.1, s32[16]{0:T(128)} %halo_send.1, s32[2,128]{1,0:T(2,128)} %bitcast.3, s32[256]{0:T(256)} %tile_src.1, ...), custom_call_target="tpu_custom_call" | custom-call | tf_op jit(solution)/shard_map/pallas_call | solution.py:327
  38.8 1.9 %copy.15 = bf16[32,8192]{1,0:T(8,128)(2,1)} copy(bf16[32,8192]{1,0:T(8,128)(2,1)} %shard_map.118) | data formatting | bytes 1048576

commit v4 on v3

--- a/solution.py
+++ b/solution.py
@@ -9,6 +9,7 @@
 
 BLOCK = 128
 GROUP = 8
+STEP = 4
 CHUNKS = 2
 MESH = pl.DeviceIdType.MESH
 
@@ -203,13 +204,14 @@
             columns[i * (BLOCK // GROUP) + k] = target[:, k * GROUP : (k + 1) * GROUP]
 
     def build(g, carry):
-        column = columns[g]
-        for j in range(GROUP):
-            match = jnp.broadcast_to(column[:, j : j + 1], square) == lane
-            hot[g * GROUP + j] = jnp.where(match, 1.0, 0.0).astype(jnp.bfloat16)
+        for i in range(2):
+            column = columns[g * 2 + i]
+            for j in range(GROUP):
+                match = jnp.broadcast_to(column[:, j : j + 1], square) == lane
+                hot[(g * 2 + i) * GROUP + j] = jnp.where(match, 1.0, 0.0).astype(jnp.bfloat16)
         return carry
 
-    lax.fori_loop(0, tiles // GROUP, build, 0)
+    lax.fori_loop(0, tiles // (2 * GROUP), build, 0)
     link_load.wait()
     for copy in copies:
         copy.wait()
@@ -218,62 +220,67 @@
     ones = jnp.ones((16, BLOCK), jnp.bfloat16)
 
     def group(g, carry):
-        first = pl.multiple_of(g * GROUP, GROUP)
-        esrc_rows = esrc[pl.ds(first, GROUP), :]
+        first = pl.multiple_of(g * (STEP * GROUP), STEP * GROUP)
         parts = []
-        for j in range(GROUP):
-            values = table[src[first + j]]
-            index = jnp.broadcast_to(esrc_rows[j : j + 1, :], values.shape)
-            picked = jnp.take_along_axis(values, index, axis=1, mode="promise_in_bounds")
-            left = jnp.concatenate([picked.astype(jnp.bfloat16), ones], axis=0)
-            parts.append(jnp.dot(left, hot[first + j], preferred_element_type=jnp.float32))
-        span = g // (BLOCK // GROUP)
-        spot = lax.rem(g, BLOCK // GROUP) * GROUP
-        for j in range(GROUP):
+        for i in range(STEP):
+            esrc_rows = esrc[pl.ds(first + i * GROUP, GROUP), :]
+            for j in range(GROUP):
+                t = first + i * GROUP + j
+                values = table[src[t]]
+                index = jnp.broadcast_to(esrc_rows[j : j + 1, :], values.shape)
+                picked = jnp.take_along_axis(values, index, axis=1, mode="promise_in_bounds")
+                left = jnp.concatenate([picked.astype(jnp.bfloat16), ones], axis=0)
+                parts.append(jnp.dot(left, hot[t], preferred_element_type=jnp.float32))
+        span = first // BLOCK
+        spot = lax.rem(first, BLOCK)
+        for j in range(STEP * GROUP):
             running[first + j + 1] = running[link[span, spot + j]] + parts[j]
         return carry
 
-    lax.fori_loop(0, tiles // GROUP, group, 0)
-
-    def quarter_means(owner):
-        def finish(i, carry):
-            b = owner * per_quarter + i
+    lax.fori_loop(0, tiles // (STEP * GROUP), group, 0)
+
+    width = quarter // CHUNKS
+    per_chunk = width // BLOCK
+
+    def chunk_means(owner, c):
+        for i in range(per_chunk):
+            b = owner * per_quarter + c * per_chunk + i
             total = running[link[spans, b]]
             degree = jnp.maximum(total[rows : rows + 1, :], 1.0)
             means[:, block_at(b)] = (total[:rows, :] / degree).astype(jnp.bfloat16)
-            return carry
-
-        lax.fori_loop(0, per_quarter, finish, 0, unroll=4)
 
     mean_rows = pl.ds(pl.multiple_of(total_rows + col * rows, rows), rows)
     mean_copies = []
-    for k, peer in enumerate(peers):
-        quarter_means(peer)
-        mean_copies.append(
-            pltpu.make_async_remote_copy(
-                src_ref=means.at[:, pl.ds(pl.multiple_of(peer * quarter, BLOCK), quarter)],
-                dst_ref=joined.at[mean_rows, :],
-                send_sem=mean_send.at[k],
-                recv_sem=mean_recv.at[k],
-                device_id=(me, peer),
-                device_id_type=MESH,
-            )
-        )
-        mean_copies[-1].start()
-    quarter_means(col)
+    for c in range(CHUNKS):
+        cols = pl.ds(c * width, width)
+        for k, peer in enumerate(peers):
+            chunk_means(peer, c)
+            spot = pl.ds(pl.multiple_of(peer * quarter + c * width, BLOCK), width)
+            mean_copies.append(
+                pltpu.make_async_remote_copy(
+                    src_ref=means.at[:, spot],
+                    dst_ref=joined.at[mean_rows, cols],
+                    send_sem=mean_send.at[c, k],
+                    recv_sem=mean_recv.at[c, k],
+                    device_id=(me, peer),
+                    device_id_type=MESH,
+                )
+            )
+            mean_copies[-1].start()
+    for c in range(CHUNKS):
+        chunk_means(col, c)
     joined[mean_rows, :] = means[:, own_nodes]
     column = jnp.transpose(jnp.broadcast_to(bias_row[...], (BLOCK, total_rows)))[:, :1]
     for copy in feat_copies:
         copy.wait()
-    for copy in mean_copies:
-        copy.wait()
-    width = quarter // CHUNKS
     out_copies = []
     own_copies = []
     for c in range(CHUNKS):
         cols = pl.ds(c * width, width)
+        for copy in mean_copies[c * len(peers) : (c + 1) * len(peers)]:
+            copy.wait()
         total = jnp.dot(weight[...], joined[:, cols], preferred_element_type=jnp.float32)
-        result[:, cols] = jnp.maximum(total + column, 0.0).astype(jnp.bfloat16)
+        result[:, cols] = (total + column).astype(jnp.bfloat16)
         place = pl.ds(pl.multiple_of(col * quarter + c * width, BLOCK), width)
         for k, peer in enumerate(peers):
             out_copies.append(
@@ -324,7 +331,7 @@
     quarter = nodes // f
     bf16, f32, i32 = jnp.bfloat16, jnp.float32, jnp.int32
     vmem, smem, dma = pltpu.VMEM, pltpu.SMEM, pltpu.SemaphoreType.DMA
-    return pl.pallas_call(
+    total = pl.pallas_call(
         functools.partial(layer_kernel, n, f),
         out_shape=jax.ShapeDtypeStruct((rows, nodes), bf16),
         in_specs=[pl.BlockSpec(memory_space=pl.ANY)] * 12,
@@ -358,8 +365,8 @@
             dma((n + 2,)),
             dma((f,)),
             dma((f,)),
-            dma((f,)),
-            dma((f,)),
+            dma((CHUNKS, f)),
+            dma((CHUNKS, f)),
             dma((CHUNKS, f)),
             dma((CHUNKS, f)),
             dma((CHUNKS,)),
@@ -381,6 +388,7 @@
         edge_src,
         edge_dst,
     )
+    return jax.nn.relu(total)
 
 
 def solution(mesh):

time: 40.9 us -> 33.2 us (0.81)
  Pallas kernels: 38.2 us -> 30.5 us
  other arithmetic: 0 us -> 1.87 us
  local copies, waits for them, and re-layouts: 1.87 us -> 0 us
    pallas_call x1, Pallas kernels: 38.2 us -> 30.5 us  [shards(): pl.pallas_call(functools.partial(layer_kernel, n, f), out_shape=jax.Shape...]
    max x0 -> x1, other arithmetic: none -> 1.87 us  [shards(): return jax.nn.relu(total)]
    unnamed x1 -> x0, local copies, waits for them, and re-layouts: 1.87 us -> none
where the time goes in v4:
time: 33.2 us; the launch traced here: 33 us
  Pallas kernels  30.5 us (92%)
  other arithmetic  1.87 us (6%)
  between operations  0.66 us (2%)
    pallas_call x1, Pallas kernels, shards(): pl.pallas_call(functools.partial(layer_kernel, n, f), out_shape=jax.Shape...  30.5 us
    max x1, other arithmetic, shards(): return jax.nn.relu(total)  1.87 us

profile of v4, /device:TPU:0, one launch (start us, length us, event | category | flops | bytes accessed | tf_op | source)
XLA Modules:
  0.0 33.0 jit_solution(9251698236632001892)
XLA Ops:
  0.7 30.5 %shard_map.118 = bf16[32,8192]{1,0:T(8,128)(2,1)} custom-call(bf16[32,8192]{1,0:T(8,128)(2,1)} %features.1, bf16[128,128]{1,0:T(8,128)(2,1)} %w_self.1, bf16[128,128]{1,0:T(8,128)(2,1)} %w_neigh.1, f32[1,128]{1,0:T(1,128)} %bitcast.5, s32[2]{0:T(128)} %hub_pick.1, s32[16]{0:T(128)} %halo_send.1, s32[2,128]{1,0:T(2,128)} %bitcast.3, s32[256]{0:T(256)} %tile_src.1, ...), custom_call_target="tpu_custom_call" | custom-call | tf_op jit(solution)/shard_map/pallas_call | solution.py:334
  31.1 1.9 %broadcast_maximum_fusion = bf16[32,8192]{1,0:T(8,128)(2,1)} fusion(bf16[32,8192]{1,0:T(8,128)(2,1)} %shard_map.118), kind=kLoop, calls=%fused_computation | loop fusion | flops 262144 | bytes 1048576 | tf_op jit(solution)/shard_map/jit(relu)/max | solution.py:391

commit v5 on v4

--- a/solution.py
+++ b/solution.py
@@ -9,8 +9,9 @@
 
 BLOCK = 128
 GROUP = 8
-STEP = 4
-CHUNKS = 2
+STEP = 8
+CHUNKS = 4
+PIECES = 4
 MESH = pl.DeviceIdType.MESH
 
 
@@ -84,6 +85,13 @@
     turns = [(a, b) for a in list(range(1, half)) + [0] for b in (0, 1) if (a, b) != (0, 0)]
     peers = [lax.rem(high + a, half) * 2 + lax.rem(low + b, 2) for a, b in turns]
 
+    barrier = pltpu.get_barrier_semaphore()
+    for k in range(1, n):
+        pl.semaphore_signal(
+            barrier, inc=1, device_id=(lax.rem(me + k, n), col), device_id_type=MESH
+        )
+    for peer in peers:
+        pl.semaphore_signal(barrier, inc=1, device_id=(me, peer), device_id_type=MESH)
     pairs = (
         (features, feat),
         (hub_pick, pick),
@@ -101,13 +109,6 @@
     loads = [pltpu.make_async_copy(a, b, local_sem.at[i]) for i, (a, b) in enumerate(pairs)]
     for load in loads:
         load.start()
-    barrier = pltpu.get_barrier_semaphore()
-    for k in range(1, n):
-        pl.semaphore_signal(
-            barrier, inc=1, device_id=(lax.rem(me + k, n), col), device_id_type=MESH
-        )
-    for peer in peers:
-        pl.semaphore_signal(barrier, inc=1, device_id=(me, peer), device_id_type=MESH)
     running[0] = jnp.zeros_like(running[0])
     for load in loads[:3]:
         load.wait()
@@ -280,7 +281,7 @@
         for copy in mean_copies[c * len(peers) : (c + 1) * len(peers)]:
             copy.wait()
         total = jnp.dot(weight[...], joined[:, cols], preferred_element_type=jnp.float32)
-        result[:, cols] = (total + column).astype(jnp.bfloat16)
+        result[:, cols] = jnp.maximum(total + column, 0.0).astype(jnp.bfloat16)
         place = pl.ds(pl.multiple_of(col * quarter + c * width, BLOCK), width)
         for k, peer in enumerate(peers):
             out_copies.append(
@@ -302,6 +303,31 @@
         own_copies[-1].start()
     for copy in out_copies + own_copies:
         copy.wait()
+
+
+def hand_on_kernel(held, out, sem):
+    width = held.shape[1] // PIECES
+    copies = [
+        pltpu.make_async_copy(
+            held.at[:, pl.ds(i * width, width)], out.at[:, pl.ds(i * width, width)], sem.at[i]
+        )
+        for i in range(PIECES)
+    ]
+    for copy in copies:
+        copy.start()
+    for copy in copies:
+        copy.wait()
+
+
+def hand_on(held):
+    return pl.pallas_call(
+        hand_on_kernel,
+        out_shape=jax.ShapeDtypeStruct(held.shape, held.dtype),
+        in_specs=[pl.BlockSpec(memory_space=pl.ANY)],
+        out_specs=pl.BlockSpec(memory_space=pl.ANY),
+        scratch_shapes=[pltpu.SemaphoreType.DMA((PIECES,))],
+        compiler_params=pltpu.CompilerParams(vmem_limit_bytes=56 * 1024 * 1024),
+    )(held)
 
 
 def shards(
@@ -388,7 +414,7 @@
         edge_src,
         edge_dst,
     )
-    return jax.nn.relu(total)
+    return hand_on(total)
 
 
 def solution(mesh):

time: 33.2 us -> 47.8 us (1.44)
  Pallas kernels: 30.5 us -> 47 us
  other arithmetic: 1.87 us -> 0 us
    pallas_call x0 -> x1, Pallas kernels: none -> 17 us  [hand_on(): pl.pallas_call(hand_on_kernel, out_shape=jax.ShapeDtypeStruct(held.shape,...]
    max x1 -> x0, other arithmetic: 1.87 us -> none  [shards(): return jax.nn.relu(total)]
    pallas_call x1, Pallas kernels: 30.5 us -> 29.9 us  [shards(): pl.pallas_call(functools.partial(layer_kernel, n, f), out_shape=jax.Shape...]
where the time goes in v5:
time: 47.8 us; the launch traced here: 47.6 us
  Pallas kernels  47 us (98%)
  between operations  0.66 us (1%)
    pallas_call x1, Pallas kernels, shards(): pl.pallas_call(functools.partial(layer_kernel, n, f), out_shape=jax.Shape...  29.9 us
    pallas_call x1, Pallas kernels, hand_on(): pl.pallas_call(hand_on_kernel, out_shape=jax.ShapeDtypeStruct(held.shape,...  17 us

profile of v5, /device:TPU:0, one launch (start us, length us, event | category | flops | bytes accessed | tf_op | source)
XLA Modules:
  0.0 47.6 jit_solution(7242905874624592785)
XLA Ops:
  0.7 29.9 %shard_map.118.held = bf16[32,8192]{1,0:T(8,128)(2,1)} custom-call(bf16[32,8192]{1,0:T(8,128)(2,1)} %features.1, bf16[128,128]{1,0:T(8,128)(2,1)} %w_self.1, bf16[128,128]{1,0:T(8,128)(2,1)} %w_neigh.1, f32[1,128]{1,0:T(1,128)} %bitcast.5, s32[2]{0:T(128)} %hub_pick.1, s32[16]{0:T(128)} %halo_send.1, s32[2,128]{1,0:T(2,128)} %bitcast.3, s32[256]{0:T(256)} %tile_src.1, ...), custom_call_target="tpu_custom_call" | custom-call | tf_op jit(solution)/shard_map/pallas_call | solution.py:360
  30.6 17.0 %shard_map.119 = bf16[32,8192]{1,0:T(8,128)(2,1)} custom-call(bf16[32,8192]{1,0:T(8,128)(2,1)} %shard_map.118.held), custom_call_target="tpu_custom_call" | custom-call | tf_op jit(solution)/shard_map/pallas_call | solution.py:323

commit v6 on v4

--- a/solution.py
+++ b/solution.py
@@ -9,8 +9,8 @@
 
 BLOCK = 128
 GROUP = 8
-STEP = 4
-CHUNKS = 2
+STEP = 8
+CHUNKS = 4
 MESH = pl.DeviceIdType.MESH
 
 
@@ -84,6 +84,13 @@
     turns = [(a, b) for a in list(range(1, half)) + [0] for b in (0, 1) if (a, b) != (0, 0)]
     peers = [lax.rem(high + a, half) * 2 + lax.rem(low + b, 2) for a, b in turns]
 
+    barrier = pltpu.get_barrier_semaphore()
+    for k in range(1, n):
+        pl.semaphore_signal(
+            barrier, inc=1, device_id=(lax.rem(me + k, n), col), device_id_type=MESH
+        )
+    for peer in peers:
+        pl.semaphore_signal(barrier, inc=1, device_id=(me, peer), device_id_type=MESH)
     pairs = (
         (features, feat),
         (hub_pick, pick),
@@ -101,13 +108,6 @@
     loads = [pltpu.make_async_copy(a, b, local_sem.at[i]) for i, (a, b) in enumerate(pairs)]
     for load in loads:
         load.start()
-    barrier = pltpu.get_barrier_semaphore()
-    for k in range(1, n):
-        pl.semaphore_signal(
-            barrier, inc=1, device_id=(lax.rem(me + k, n), col), device_id_type=MESH
-        )
-    for peer in peers:
-        pl.semaphore_signal(barrier, inc=1, device_id=(me, peer), device_id_type=MESH)
     running[0] = jnp.zeros_like(running[0])
     for load in loads[:3]:
         load.wait()
@@ -280,7 +280,7 @@
         for copy in mean_copies[c * len(peers) : (c + 1) * len(peers)]:
             copy.wait()
         total = jnp.dot(weight[...], joined[:, cols], preferred_element_type=jnp.float32)
-        result[:, cols] = (total + column).astype(jnp.bfloat16)
+        result[:, cols] = jnp.maximum(total + column, 0.0).astype(jnp.bfloat16)
         place = pl.ds(pl.multiple_of(col * quarter + c * width, BLOCK), width)
         for k, peer in enumerate(peers):
             out_copies.append(
@@ -331,11 +331,11 @@
     quarter = nodes // f
     bf16, f32, i32 = jnp.bfloat16, jnp.float32, jnp.int32
     vmem, smem, dma = pltpu.VMEM, pltpu.SMEM, pltpu.SemaphoreType.DMA
-    total = pl.pallas_call(
+    return pl.pallas_call(
         functools.partial(layer_kernel, n, f),
-        out_shape=jax.ShapeDtypeStruct((rows, nodes), bf16),
+        out_shape=vmem((rows, nodes), bf16),
         in_specs=[pl.BlockSpec(memory_space=pl.ANY)] * 12,
-        out_specs=pl.BlockSpec(memory_space=pl.ANY),
+        out_specs=pl.BlockSpec(memory_space=pltpu.VMEM),
         scratch_shapes=[
             vmem((rows, nodes), bf16),
             vmem((full, 2 * full), bf16),
@@ -388,7 +388,6 @@
         edge_src,
         edge_dst,
     )
-    return jax.nn.relu(total)
 
 
 def solution(mesh):

time: 33.2 us -> 31.4 us (0.946)
  other arithmetic: 1.87 us -> 0 us
  local copies, waits for them, and re-layouts: 0 us -> 0.8 us
  Pallas kernels: 30.5 us -> 29.8 us
    max x1 -> x0, other arithmetic: 1.87 us -> none  [shards(): return jax.nn.relu(total)]
    unnamed x0 -> x1, local copies, waits for them, and re-layouts: none -> 0.8 us
    pallas_call x1, Pallas kernels: 30.5 us -> 29.8 us  [shards(): pl.pallas_call(functools.partial(layer_kernel, n, f), out_shape=vmem((row...]
where the time goes in v6:
time: 31.4 us; the launch traced here: 31.3 us
  Pallas kernels  29.8 us (95%)
  local copies, waits for them, and re-layouts  0.8 us (3%)
  between operations  0.66 us (2%)
    pallas_call x1, Pallas kernels, shards(): pl.pallas_call(functools.partial(layer_kernel, n, f), out_shape=vmem((row...  29.8 us
    unnamed x1, local copies, waits for them, and re-layouts  0.8 us

profile of v6, /device:TPU:0, one launch (start us, length us, event | category | flops | bytes accessed | tf_op | source)
XLA Modules:
  0.0 31.3 jit_solution(12249165378665474580)
XLA Ops:
  0.7 29.8 %shard_map.118 = bf16[32,8192]{1,0:T(8,128)(2,1)S(1)} custom-call(bf16[32,8192]{1,0:T(8,128)(2,1)} %features.1, bf16[128,128]{1,0:T(8,128)(2,1)} %w_self.1, bf16[128,128]{1,0:T(8,128)(2,1)} %w_neigh.1, f32[1,128]{1,0:T(1,128)} %bitcast.5, s32[2]{0:T(128)} %hub_pick.1, s32[16]{0:T(128)} %halo_send.1, s32[2,128]{1,0:T(2,128)} %bitcast.3, s32[256]{0:T(256)} %tile_src.1, ...), custom_call_target="tpu_custom_call" | custom-call | tf_op jit(solution)/shard_map/pallas_call | solution.py:334
  30.5 0.8 %copy.14 = bf16[32,8192]{1,0:T(8,128)(2,1)} copy(bf16[32,8192]{1,0:T(8,128)(2,1)S(1)} %shard_map.118) | data formatting | bytes 1048576

commit v7 on v6

--- a/solution.py
+++ b/solution.py
@@ -230,7 +230,8 @@
                 index = jnp.broadcast_to(esrc_rows[j : j + 1, :], values.shape)
                 picked = jnp.take_along_axis(values, index, axis=1, mode="promise_in_bounds")
                 left = jnp.concatenate([picked.astype(jnp.bfloat16), ones], axis=0)
-                parts.append(jnp.dot(left, hot[t], preferred_element_type=jnp.float32))
+                part = jnp.dot(left, hot[t], preferred_element_type=jnp.float32)
+                parts.append(part[: rows + 8])
         span = first // BLOCK
         spot = lax.rem(first, BLOCK)
         for j in range(STEP * GROUP):
@@ -356,7 +357,7 @@
             vmem((rows, hub_per * BLOCK), bf16),
             vmem((rows, 2 * halo * BLOCK), bf16),
             vmem((rows, extra * BLOCK), bf16),
-            vmem((tiles + 1, rows + 16, BLOCK), f32),
+            vmem((tiles + 1, rows + 8, BLOCK), f32),
             vmem((rows, nodes), bf16),
             vmem((2 * full, quarter), bf16),
             vmem((full, quarter), bf16),

time: 31.4 us -> 31.4 us (level)
  no operation moved by 1% of the time
where the time goes in v7:
time: 31.4 us; the launch traced here: 31.2 us
  Pallas kernels  29.8 us (95%)
  local copies, waits for them, and re-layouts  0.8 us (3%)
  between operations  0.66 us (2%)
    pallas_call x1, Pallas kernels, shards(): pl.pallas_call(functools.partial(layer_kernel, n, f), out_shape=vmem((row...  29.8 us
    unnamed x1, local copies, waits for them, and re-layouts  0.8 us

profile of v7, /device:TPU:0, one launch (start us, length us, event | category | flops | bytes accessed | tf_op | source)
XLA Modules:
  0.0 31.2 jit_solution(6753820706507118350)
XLA Ops:
  0.7 29.8 %shard_map.118 = bf16[32,8192]{1,0:T(8,128)(2,1)S(1)} custom-call(bf16[32,8192]{1,0:T(8,128)(2,1)} %features.1, bf16[128,128]{1,0:T(8,128)(2,1)} %w_self.1, bf16[128,128]{1,0:T(8,128)(2,1)} %w_neigh.1, f32[1,128]{1,0:T(1,128)} %bitcast.5, s32[2]{0:T(128)} %hub_pick.1, s32[16]{0:T(128)} %halo_send.1, s32[2,128]{1,0:T(2,128)} %bitcast.3, s32[256]{0:T(256)} %tile_src.1, ...), custom_call_target="tpu_custom_call" | custom-call | tf_op jit(solution)/shard_map/pallas_call | solution.py:335
  30.4 0.8 %copy.14 = bf16[32,8192]{1,0:T(8,128)(2,1)} copy(bf16[32,8192]{1,0:T(8,128)(2,1)S(1)} %shard_map.118) | data formatting | bytes 1048576

commit v8 on v7

--- a/solution.py
+++ b/solution.py
@@ -16,6 +16,23 @@
 
 def block_at(index):
     return pl.ds(pl.multiple_of(index * BLOCK, BLOCK), BLOCK)
+
+
+def lane_gather(values, index):
+    numbers = lax.GatherDimensionNumbers(
+        offset_dims=(),
+        collapsed_slice_dims=(1,),
+        start_index_map=(1,),
+        operand_batching_dims=(0,),
+        start_indices_batching_dims=(0,),
+    )
+    return lax.gather(
+        values,
+        index[..., None],
+        numbers,
+        slice_sizes=(1, 1),
+        mode=lax.GatherScatterMode.PROMISE_IN_BOUNDS,
+    )
 
 
 def layer_kernel(
@@ -112,11 +129,11 @@
     for load in loads[:3]:
         load.wait()
     for b in range(blocks):
-        table[b] = feat[:, b * BLOCK : (b + 1) * BLOCK].astype(jnp.float32)
+        table[b] = feat[:, b * BLOCK : (b + 1) * BLOCK]
     for j in range(2 * halo):
-        halo_buf[:, j * BLOCK : (j + 1) * BLOCK] = table[send[j]].astype(jnp.bfloat16)
+        halo_buf[:, j * BLOCK : (j + 1) * BLOCK] = table[send[j]]
     for j in range(hub_per):
-        hub_buf[:, j * BLOCK : (j + 1) * BLOCK] = table[pick[j]].astype(jnp.bfloat16)
+        hub_buf[:, j * BLOCK : (j + 1) * BLOCK] = table[pick[j]]
     hub_cols = hub_per * BLOCK
     halo_cols = halo * BLOCK
     own_hubs = pl.ds(pl.multiple_of(me * hub_cols, BLOCK), hub_cols)
@@ -216,7 +233,7 @@
     for copy in copies:
         copy.wait()
     for b in range(ext.shape[1] // BLOCK):
-        table[blocks + b] = ext[:, b * BLOCK : (b + 1) * BLOCK].astype(jnp.float32)
+        table[blocks + b] = ext[:, b * BLOCK : (b + 1) * BLOCK]
     ones = jnp.ones((16, BLOCK), jnp.bfloat16)
 
     def group(g, carry):
@@ -227,9 +244,9 @@
             for j in range(GROUP):
                 t = first + i * GROUP + j
                 values = table[src[t]]
-                index = jnp.broadcast_to(esrc_rows[j : j + 1, :], values.shape)
-                picked = jnp.take_along_axis(values, index, axis=1, mode="promise_in_bounds")
-                left = jnp.concatenate([picked.astype(jnp.bfloat16), ones], axis=0)
+                index = jnp.broadcast_to(esrc_rows[j : j + 1, :], values.shape).astype(jnp.int16)
+                picked = lane_gather(values, index)
+                left = jnp.concatenate([picked, ones], axis=0)
                 part = jnp.dot(left, hot[t], preferred_element_type=jnp.float32)
                 parts.append(part[: rows + 8])
         span = first // BLOCK
@@ -353,7 +370,7 @@
             smem((8, BLOCK), i32),
             vmem((tiles // GROUP, BLOCK, GROUP), f32),
             vmem((tiles, BLOCK, BLOCK), bf16),
-            vmem((blocks + extra, rows, BLOCK), f32),
+            vmem((blocks + extra, rows, BLOCK), bf16),
             vmem((rows, hub_per * BLOCK), bf16),
             vmem((rows, 2 * halo * BLOCK), bf16),
             vmem((rows, extra * BLOCK), bf16),

time: 31.4 us -> 31.4 us (level)
  no operation moved by 1% of the time
where the time goes in v8:
time: 31.4 us; the launch traced here: 31.3 us
  Pallas kernels  29.8 us (95%)
  local copies, waits for them, and re-layouts  0.8 us (3%)
  between operations  0.66 us (2%)
    pallas_call x1, Pallas kernels, shards(): pl.pallas_call(functools.partial(layer_kernel, n, f), out_shape=vmem((row...  29.8 us
    unnamed x1, local copies, waits for them, and re-layouts  0.8 us

profile of v8, /device:TPU:0, one launch (start us, length us, event | category | flops | bytes accessed | tf_op | source)
XLA Modules:
  0.0 31.3 jit_solution(15377553148442110890)
XLA Ops:
  0.7 29.8 %shard_map.118 = bf16[32,8192]{1,0:T(8,128)(2,1)S(1)} custom-call(bf16[32,8192]{1,0:T(8,128)(2,1)} %features.1, bf16[128,128]{1,0:T(8,128)(2,1)} %w_self.1, bf16[128,128]{1,0:T(8,128)(2,1)} %w_neigh.1, f32[1,128]{1,0:T(1,128)} %bitcast.5, s32[2]{0:T(128)} %hub_pick.1, s32[16]{0:T(128)} %halo_send.1, s32[2,128]{1,0:T(2,128)} %bitcast.3, s32[256]{0:T(256)} %tile_src.1, ...), custom_call_target="tpu_custom_call" | custom-call | tf_op jit(solution)/shard_map/pallas_call | solution.py:352
  30.5 0.8 %copy.14 = bf16[32,8192]{1,0:T(8,128)(2,1)} copy(bf16[32,8192]{1,0:T(8,128)(2,1)S(1)} %shard_map.118) | data formatting | bytes 1048576

commit v9 on v8

--- a/solution.py
+++ b/solution.py
@@ -179,7 +179,6 @@
                 device_id_type=MESH,
             )
         )
-        feat_copies[-1].start()
     joined[own_rows, :] = feat[:, own_nodes]
     ext[:, own_hubs] = hub_buf[...]
     for load in loads[3:]:
@@ -230,8 +229,10 @@
 
     lax.fori_loop(0, tiles // (2 * GROUP), build, 0)
     link_load.wait()
+    for copy in feat_copies:
+        copy.start()
     for copy in copies:
-        copy.wait()
+        copy.wait_recv()
     for b in range(ext.shape[1] // BLOCK):
         table[blocks + b] = ext[:, b * BLOCK : (b + 1) * BLOCK]
     ones = jnp.ones((16, BLOCK), jnp.bfloat16)
@@ -290,13 +291,13 @@
     joined[mean_rows, :] = means[:, own_nodes]
     column = jnp.transpose(jnp.broadcast_to(bias_row[...], (BLOCK, total_rows)))[:, :1]
     for copy in feat_copies:
-        copy.wait()
+        copy.wait_recv()
     out_copies = []
     own_copies = []
     for c in range(CHUNKS):
         cols = pl.ds(c * width, width)
         for copy in mean_copies[c * len(peers) : (c + 1) * len(peers)]:
-            copy.wait()
+            copy.wait_recv()
         total = jnp.dot(weight[...], joined[:, cols], preferred_element_type=jnp.float32)
         result[:, cols] = jnp.maximum(total + column, 0.0).astype(jnp.bfloat16)
         place = pl.ds(pl.multiple_of(col * quarter + c * width, BLOCK), width)
@@ -318,6 +319,8 @@
             )
         )
         own_copies[-1].start()
+    for copy in copies + feat_copies + mean_copies:
+        copy.wait_send()
     for copy in out_copies + own_copies:
         copy.wait()
 

time: 31.4 us -> 33.6 us (1.070)
  Pallas kernels: 29.8 us -> 32 us
    pallas_call x1, Pallas kernels: 29.8 us -> 32 us  [shards(): pl.pallas_call(functools.partial(layer_kernel, n, f), out_shape=vmem((row...]
where the time goes in v9:
time: 33.6 us; the launch traced here: 33.5 us
  Pallas kernels  32 us (95%)
  local copies, waits for them, and re-layouts  0.8 us (2%)
  between operations  0.66 us (2%)
    pallas_call x1, Pallas kernels, shards(): pl.pallas_call(functools.partial(layer_kernel, n, f), out_shape=vmem((row...  32 us
    unnamed x1, local copies, waits for them, and re-layouts  0.8 us

profile of v9, /device:TPU:0, one launch (start us, length us, event | category | flops | bytes accessed | tf_op | source)
XLA Modules:
  0.0 33.5 jit_solution(14824026983244373896)
XLA Ops:
  0.7 32.0 %shard_map.118 = bf16[32,8192]{1,0:T(8,128)(2,1)S(1)} custom-call(bf16[32,8192]{1,0:T(8,128)(2,1)} %features.1, bf16[128,128]{1,0:T(8,128)(2,1)} %w_self.1, bf16[128,128]{1,0:T(8,128)(2,1)} %w_neigh.1, f32[1,128]{1,0:T(1,128)} %bitcast.5, s32[2]{0:T(128)} %hub_pick.1, s32[16]{0:T(128)} %halo_send.1, s32[2,128]{1,0:T(2,128)} %bitcast.3, s32[256]{0:T(256)} %tile_src.1, ...), custom_call_target="tpu_custom_call" | custom-call | tf_op jit(solution)/shard_map/pallas_call | solution.py:355
  32.7 0.8 %copy.14 = bf16[32,8192]{1,0:T(8,128)(2,1)} copy(bf16[32,8192]{1,0:T(8,128)(2,1)S(1)} %shard_map.118) | data formatting | bytes 1048576
